TPU v7x, 32 devices: a whole 2x2x4 slice. The times are simulated.
32 devices in a mesh: row: 4 (over y, x), col: 8 (over z, core).
Axes of the slice: x: 2, y: 2, z: 4, core: 2. Of those that a mesh axis runs over, the one named last changes fastest.
Arguments:
- l_rows: float32 [4096, 4096], P('row', 'col'), may hold values from -6 to 6
- v_prev: float32 [4096, 1024], P('col', 'row'), may hold values from -0.09375 to 0.09375
- l_tail: float32 [4096, 4096], P('row', 'col'), may hold values from -5 to 100, as said below
- k_cross: float32 [4096, 1024], P('row', 'col'), may hold values from -6 to 6
- k_query: float32 [1024, 1024], P('row', 'col'), may hold values from -2 to 5, as said below
Outputs:
- tail_solution: float32 [4096, 1024], P('row', 'col')
- posterior: float32 [1024, 1024], P('row', 'col')
Inputs may be any that keep to these rules, and one draw needn't show every extreme that they name: `l_tail`: lower triangular; its diagonal lies between 40 and 100. `k_query`: symmetric.
All inputs are finite; a program needn't handle non-finite values.
Results may differ from a plain program's by a relative error of at most 0.000076.
Values sent between devices are 32-bit elements; how exact they have to be, the bound alone decides.
A program may use at most 64 MiB of HBM per device.

v0:
```python
import jax
import jax.numpy as jnp
from jax import lax
from jax.sharding import PartitionSpec as P


def spread(value, axis, root):
    mine = lax.axis_index(axis) == root
    return lax.psum(jnp.where(mine, value, jnp.zeros_like(value)), axis)


def body(l_rows, v_prev, l_tail, k_cross, k_query):
    highest = lax.Precision.HIGHEST
    tail_rows = l_rows.shape[0]
    shard_piece = lax.all_gather(v_prev, "row", axis=1, tiled=True)
    update = jnp.dot(l_rows, shard_piece, precision=highest, preferred_element_type=jnp.float32)
    own_gram = jnp.dot(v_prev.T, shard_piece, precision=highest, preferred_element_type=jnp.float32)
    partial_value = jnp.concatenate([update, own_gram], axis=0)
    summed = lax.psum_scatter(partial_value, "col", scatter_dimension=1, tiled=True)
    residual = k_cross - summed[:tail_rows]
    gram_prior = summed[tail_rows:]
    factor = lax.all_gather(l_tail, "col", axis=1, tiled=True)
    row_index = lax.axis_index("row")
    row_count = lax.axis_size("row")
    diagonal_block = lax.dynamic_slice_in_dim(factor, row_index * tail_rows, tail_rows, 1)
    query_cols = residual.shape[1]
    empty_block = jnp.zeros((tail_rows, query_cols), jnp.float32)

    def solve_block(right_side):
        return jax.scipy.linalg.solve_triangular(diagonal_block, right_side, lower=True)

    def advance(turn_index, carry):
        pending, own_block = carry
        candidate = lax.cond(
            turn_index == row_index, lambda: solve_block(residual - pending), lambda: own_block
        )
        solved = spread(candidate, "row", turn_index)
        columns = lax.dynamic_slice_in_dim(factor, turn_index * tail_rows, tail_rows, 1)
        pending = pending + jnp.dot(
            columns, solved, precision=highest, preferred_element_type=jnp.float32
        )
        own_block = jnp.where(turn_index == row_index, solved, own_block)
        return (pending, own_block)

    pending, own_block = lax.fori_loop(0, row_count, advance, (empty_block, empty_block))
    cross_gram = jnp.dot(
        own_block.T,
        lax.all_gather(own_block, "col", axis=1, tiled=True),
        precision=highest,
        preferred_element_type=jnp.float32,
    )
    gram_tail = lax.psum_scatter(cross_gram, "row", scatter_dimension=1, tiled=True)
    posterior = k_query - gram_prior - gram_tail.T
    return (own_block, posterior)


def solution(mesh):
    in_specs = (P("row", "col"), P("col", "row"), P("row", "col"), P("row", "col"), P("row", "col"))
    out_specs = (P("row", "col"), P("row", "col"))
    return jax.shard_map(body, mesh=mesh, in_specs=in_specs, out_specs=out_specs, check_vma=False)
```

profile of v0, /device:TPU:0, one launch (start us, length us, event | category | flops | bytes accessed | tf_op | source)
XLA Modules:
  0.0 1125.8 jit_solution(11220533524885605545)
XLA Ops:
  8.0 39.8 %all-gather.6.cloned.1.call-done = f32[512,1024]{1,0:T(8,128)} async-done(((f32[512,256]{1,0:T(8,128)}), f32[512,1024]{1,0:T(8,128)}) %all-gather.6.cloned.1.call-update) | async-done | bytes 2097168 | tf_op jit(solution)/shard_map/all_gather | solution.py:15
  47.7 3.8 fusion.43
  51.5 6.9 fusion.42
  58.4 3.2 pad_maximum_fusion
  62.4 59.3 %reduce-scatter.3.cloned.1.call-done = f32[1280,128]{1,0:T(8,128)} async-done(((f32[1280,1024]{1,0:T(8,128)}), f32[1280,128]{1,0:T(8,128)}) %reduce-scatter.3.cloned.1.call-update) | async-done | bytes 655376 | tf_op jit(solution)/shard_map/reduce_scatter | solution.py:19
  123.6 149.2 %all-gather.4.cloned.1.call-done = f32[1024,4096]{1,0:T(8,128)} async-done(((f32[1024,512]{1,0:T(8,128)}), f32[1024,4096]{1,0:T(8,128)}) %all-gather.4.cloned.1.call-update) | async-done | bytes 16777232 | tf_op jit(solution)/shard_map/all_gather | solution.py:22
  272.8 4.7 constant_dynamic-slice_fusion.1
  277.5 755.2 %while.21 = (s32[]{:T(128)}, f32[1024,128]{1,0:T(8,128)}, f32[1024,128]{1,0:T(8,128)}, f32[1024,4096]{1,0:T(8,128)}, s32[]{:T(128)}, /*index=5*/f32[1024,1024]{1...) while((s32[]{:T(128)}, f32[1024,128]{1,0:T(8,128)}, ...), condition=%wide.region_5.6_spmd.clone, body=%wide.region_1.5_spmd.clone.sunk | while | flops 2520039424 | bytes 33425496 | solution.py:45
  277.6 134.0 %conditional.3 = (f32[1024,128]{1,0:T(8,128)}) conditional(s32[]{:T(128)} %convert_element_type.9, f32[1024,128]{1,0:T(8,128)S(1)} %get-tuple-element.300, (f32[1024,1024]{1,0:T(8,128)}, f32[1024,128]{1,0:T(8,128)}, f32[1024,128]{1,0:T(8,128)S(1)}) %tuple.85), branch_computations={%region_2.0_spmd, %region_3.3_spmd} | conditional | flops 908640256 | bytes 19793716 | solution.py:34
  277.6 4.8 fusion
  282.4 28.7 %while.20 = (s32[]{:T(128)}, f32[1024,1024]{1,0:T(8,128)}, s32[8,2]{0,1:T(2,128)S(1)}, f32[8,128,128]{2,1,0:T(8,128)}, s32[]{:T(128)}) while((s32[]{:T(128)}, f32[1024,1024]{1,0:T(8,128)}, s32[8,2]{0,1:T(2,128)S(1)}, f32[8,128,128]{2,1,0:T(8,128)}, s32[]{:T(128)}) %tuple.88), condition=%wide.while_cond, body=%wide.while_body.sunk | while | flops 2 | bytes 132705 | solution.py:30
  297.5 2.9 bitcast_dynamic-update-slice_fusion.2
  311.2 80.0 %custom-call.3 = f32[8,128,128]{1,2,0:T(8,128)} custom-call(f32[8,128,128]{2,1,0:T(8,128)} %get-tuple-element.151), custom_call_target="InvertDiagBlocksLowerTriangular" | custom-call | tf_op jit(solution)/shard_map/while/body/eval_jaxpr/cond/branch_1_fun/jit(_solve_triangular)/triangular_solve | solution.py:30
  413.5 41.9 %all-reduce.2.cloned.1.call-done = f32[1024,128]{1,0:T(8,128)} async-done(((f32[1024,128]{1,0:T(8,128)}), f32[1024,128]{1,0:T(8,128)}) %all-reduce.2.cloned.1.call-update) | async-done | bytes 524304 | tf_op jit(solution)/shard_map/while/body/eval_jaxpr/psum | solution.py:9
  457.3 6.5 fusion.69
  466.8 178.6 %all-reduce.2.cloned.1.call-done = f32[1024,128]{1,0:T(8,128)} async-done(((f32[1024,128]{1,0:T(8,128)}), f32[1024,128]{1,0:T(8,128)}) %all-reduce.2.cloned.1.call-update) | async-done | bytes 524304 | tf_op jit(solution)/shard_map/while/body/eval_jaxpr/psum | solution.py:9
  646.3 6.5 fusion.69
  655.7 179.6 %all-reduce.2.cloned.1.call-done = f32[1024,128]{1,0:T(8,128)} async-done(((f32[1024,128]{1,0:T(8,128)}), f32[1024,128]{1,0:T(8,128)}) %all-reduce.2.cloned.1.call-update) | async-done | bytes 524304 | tf_op jit(solution)/shard_map/while/body/eval_jaxpr/psum | solution.py:9
  836.2 6.5 fusion.69
  845.7 179.7 %all-reduce.2.cloned.1.call-done = f32[1024,128]{1,0:T(8,128)} async-done(((f32[1024,128]{1,0:T(8,128)}), f32[1024,128]{1,0:T(8,128)}) %all-reduce.2.cloned.1.call-update) | async-done | bytes 524304 | tf_op jit(solution)/shard_map/while/body/eval_jaxpr/psum | solution.py:9
  1026.2 6.5 fusion.69
  1033.7 50.9 %all-gather.8.cloned.1.call-done = f32[1024,1024]{1,0:T(8,128)} async-done(((f32[1024,128]{1,0:T(8,128)}), f32[1024,1024]{1,0:T(8,128)}) %all-gather.8.cloned.1.call-update) | async-done | bytes 4194320 | tf_op jit(solution)/shard_map/all_gather | solution.py:48
  1084.6 9.8 fusion.44
  1094.4 23.2 %reduce-scatter.5.cloned.1.call-done = f32[128,256]{0,1:T(8,128)} async-done(((f32[128,1024]{0,1:T(8,128)}), f32[128,256]{0,1:T(8,128)}) %reduce-scatter.5.cloned.1.call-update) | async-done | bytes 131088 | tf_op jit(solution)/shard_map/reduce_scatter | solution.py:52
  (92 shorter events, 69.8 us)
Async XLA Ops:
  7.2 44.3 %copy-start = (f32[1024,512]{1,0:T(8,128)S(1)}, f32[1024,512]{1,0:T(8,128)}, u32[]{:S(2)}) copy-start(f32[1024,512]{1,0:T(8,128)} %param.9) | copy-start | bytes 6291460
  7.2 40.6 %all-gather.6.cloned.1.call-start = ((), (), s32[]{:S(2)}) async-start(), calls=%async_computation.3 | async-start | bytes 2621440 | tf_op jit(solution)/shard_map/all_gather | solution.py:15
  7.9 113.8 %reduce-scatter.3.cloned.1.call-start = ((), (), s32[]{:S(2)}) async-start(), calls=%async_computation.4 | async-start | bytes 5898240 | tf_op jit(solution)/shard_map/reduce_scatter | solution.py:19
  47.7 3.8 copy-start.2
  61.6 60.1 %copy-start.3 = (f32[1024,128]{1,0:T(8,128)S(1)}, f32[1024,128]{1,0:T(8,128)}, u32[]{:S(2)}) copy-start(f32[1024,128]{1,0:T(8,128)} %param.12) | copy-start | bytes 1572868
  61.6 211.2 %all-gather.4.cloned.1.call-start = ((), (), s32[]{:S(2)}) async-start(), calls=%async_computation.2 | async-start | bytes 18874368 | tf_op jit(solution)/shard_map/all_gather | solution.py:22
  277.5 177.8 %all-reduce.2.cloned.1.call-start = ((), (), s32[]{:S(2)}) async-start(), calls=%async_computation.7 | async-start | bytes 1048576 | tf_op jit(solution)/shard_map/while/body/eval_jaxpr/psum | solution.py:9
  391.2 9.9 copy-start.1
  463.8 181.6 %all-reduce.2.cloned.1.call-start = ((), (), s32[]{:S(2)}) async-start(), calls=%async_computation.7 | async-start | bytes 1048576 | tf_op jit(solution)/shard_map/while/body/eval_jaxpr/psum | solution.py:9
  652.8 182.5 %all-reduce.2.cloned.1.call-start = ((), (), s32[]{:S(2)}) async-start(), calls=%async_computation.7 | async-start | bytes 1048576 | tf_op jit(solution)/shard_map/while/body/eval_jaxpr/psum | solution.py:9
  842.7 182.6 %all-reduce.2.cloned.1.call-start = ((), (), s32[]{:S(2)}) async-start(), calls=%async_computation.7 | async-start | bytes 1048576 | tf_op jit(solution)/shard_map/while/body/eval_jaxpr/psum | solution.py:9
  1032.7 84.9 %copy-start.4 = (f32[256,128]{1,0:T(8,128)S(1)}, f32[256,128]{1,0:T(8,128)}, u32[]{:S(2)}) copy-start(f32[256,128]{1,0:T(8,128)} %param.13) | copy-start | bytes 393220
  1032.7 51.9 %all-gather.8.cloned.1.call-start = ((), (), s32[]{:S(2)}) async-start(), calls=%async_computation.5 | async-start | bytes 4718592 | tf_op jit(solution)/shard_map/all_gather | solution.py:48
  1033.5 84.1 %reduce-scatter.5.cloned.1.call-start = ((), (), s32[]{:S(2)}) async-start(), calls=%async_computation.6 | async-start | bytes 655360 | tf_op jit(solution)/shard_map/reduce_scatter | solution.py:52
Sparse Core Ops, SparseCore 0:
  9.8 37.8 all-gather.5
  61.8 59.9 reduce-scatter.2
  123.3 149.4 all-gather.3
  413.6 41.7 all-reduce.1
  468.2 177.1 all-reduce.1
  657.1 178.1 all-reduce.1
  847.4 177.9 all-reduce.1
  1035.7 48.8 all-gather.7
  1094.6 23.0 reduce-scatter.4
where the time goes:
time: 1130 us
  waiting for transfers between devices  904 us (80%)
  other arithmetic  105 us (9%)
  matrix products  65.8 us (6%)
  local copies, waits for them, and re-layouts  35.8 us (3%)
  between operations  13.8 us (1%)
    psum x4, waiting for transfers between devices, spread(): return lax.psum(jnp.where(mine, value, jnp.zeros_like(value)), axis)  580 us
    all_gather x1, waiting for transfers between devices, body(): factor = lax.all_gather(l_tail, 'col', axis=1, tiled=True)  149 us
    another operation x3, other arithmetic, solve_block(): jax.scipy.linalg.solve_triangular(diagonal_block, right_side, lower=True)  84.8 us
    reduce_scatter x1, waiting for transfers between devices, body(): lax.psum_scatter(partial_value, 'col', scatter_dimension=1, tiled=True)  59.3 us
    all_gather x1, waiting for transfers between devices, body(): lax.all_gather(own_block, 'col', axis=1, tiled=True)  50.9 us
    all_gather x1, waiting for transfers between devices, body(): shard_piece = lax.all_gather(v_prev, 'row', axis=1, tiled=True)  39.8 us
    another operation x24, local copies, waits for them, and re-layouts  28.7 us
    dot_general x4, matrix products, advance(): jnp.dot(columns, solved, precision=highest, preferred_element_type=jnp.fl...  26.1 us
  transfers between devices with their start and end apart: 9, of which 9 were waited for; matrix products, arithmetic and copies ran while one was open for 0% of the time, Pallas kernels for 0%

commit v1 on v0

v1 whole, which is shorter than its diff:
```python
import functools

import jax
import jax.numpy as jnp
from jax import lax
from jax.experimental import pallas as pl
from jax.experimental.pallas import tpu as pltpu
from jax.sharding import PartitionSpec as P

F32 = jnp.float32
BF16 = jnp.bfloat16
MESH = pl.DeviceIdType.MESH


def split(value):
    high = value.astype(BF16)
    return high, (value - high.astype(F32)).astype(BF16)


def dot3(high, low, value):
    value_high, value_low = split(value)
    total = jnp.dot(high, value_high, preferred_element_type=F32)
    total += jnp.dot(high, value_low, preferred_element_type=F32)
    return total + jnp.dot(low, value_high, preferred_element_type=F32)


def exact_dot(a, b):
    return jnp.dot(a, b, precision=lax.Precision.HIGHEST, preferred_element_type=F32)


def invert_kernel(base, block_ref, out_ref):
    order = block_ref.shape[0]
    rows = lax.broadcasted_iota(jnp.int32, (base, base), 0)
    cols = lax.broadcasted_iota(jnp.int32, (base, base), 1)
    blocks = [block_ref[pl.ds(i, base), pl.ds(i, base)] for i in range(0, order, base)]
    inverses = [jnp.where(rows == cols, 1.0 / block, 0.0) for block in blocks]
    size = 1
    while size < base:
        pair = ((rows // size) % 2 == 1) & (cols // size == rows // size - 1)
        lefts = [exact_dot(inv, jnp.where(pair, block, 0.0)) for inv, block in zip(inverses, blocks)]
        inverses = [inv - exact_dot(left, inv) for inv, left in zip(inverses, lefts)]
        size *= 2
    out_ref[...] = jnp.zeros_like(out_ref)
    for i, inv in enumerate(inverses):
        out_ref[pl.ds(i * base, base), pl.ds(i * base, base)] = inv
    while size < order:
        for i in range(0, order, 2 * size):
            first, second = pl.ds(i, size), pl.ds(i + size, size)
            left = exact_dot(out_ref[second, second], block_ref[second, first])
            out_ref[second, first] = -exact_dot(left, out_ref[first, first])
        size *= 2


def invert(block):
    order = block.shape[0]
    return pl.pallas_call(
        functools.partial(invert_kernel, min(order, 128)),
        out_shape=jax.ShapeDtypeStruct(block.shape, F32),
        in_specs=[pl.BlockSpec(memory_space=pltpu.VMEM)],
        out_specs=pl.BlockSpec(memory_space=pltpu.VMEM),
        compiler_params=pltpu.CompilerParams(vmem_limit_bytes=32 * 2**20),
        cost_estimate=pl.CostEstimate(flops=20 * order**3, bytes_accessed=8 * order * order, transcendentals=0),
    )(block)


def solve_kernel(
    nr, nc, lr_ref, v_ref, lt_ref, inv_ref, kc_ref, out_ref, panel_ref,
    rh, rl, lh, ll, ih, il, s, ex, fin, back, xs, fo, xo,
    ex_s, ex_r, c_s, f_r, b_r, x_s, x_r, o_s, o_r,
):
    r, c = lax.axis_index("row"), lax.axis_index("col")
    h = xs.shape[1]
    z, k = c // 2, c % 2
    planes = nc // 2
    partner = c + 1 - 2 * k
    mine = pl.ds(pl.multiple_of(k * h, h), h)
    other = pl.ds(pl.multiple_of((1 - k) * h, h), h)

    barrier = pltpu.get_barrier_semaphore()

    @pl.loop(1, nr)
    def _(i):
        pl.semaphore_signal(barrier, inc=1, device_id=((r + i) % nr, c), device_id_type=MESH)

    @pl.loop(1, nc)
    def _(i):
        pl.semaphore_signal(barrier, inc=1, device_id=(r, (c + i) % nc), device_id_type=MESH)

    pl.semaphore_wait(barrier, nr + nc - 2)

    def remote(src, dst, send, recv, device):
        return pltpu.make_async_remote_copy(
            src_ref=src, dst_ref=dst, send_sem=send, recv_sem=recv, device_id=device, device_id_type=MESH
        )

    def exchange(q):
        return remote(s.at[q, other], ex.at[q], ex_s.at[q], ex_r.at[q], (r, partner))

    def chain(q, dst, recv, target):
        return remote(fo.at[q], dst.at[q], c_s.at[q], recv.at[q], (r, target))

    def share(i, q):
        return remote(xs.at[q], xs.at[q], x_s.at[i, q], x_r.at[q], ((r + i) % nr, c))

    def deliver(q, target):
        return remote(xs.at[q], xo.at[mine], o_s.at[q], o_r.at[k], (r, target))

    rh[...], rl[...] = split(lr_ref[...])

    @pl.loop(0, nc)
    def _(q):
        s[q] = dot3(rh[...], rl[...], v_ref[q])

        @pl.when(q == c)
        def _():
            s[q] = s[q] - kc_ref[...]

        @pl.when((z > r) | ((z == r) & (k == 1)))
        def _():
            exchange(q).start()

        @pl.when(z > r)
        def _():
            exchange(q).wait_recv()
            fo[q] = s[q, mine] + ex[q]

            @pl.when(z < planes - 1)
            def _():
                chain(q, back, b_r, partner).wait_recv()
                fo[q] = fo[q] + back[q]

            chain(q, back, b_r, c - 2).start()

    @pl.when(z <= r)
    def _():
        lh[...], ll[...] = split(lt_ref[...])

    @pl.when(z == r)
    def _():
        ih[...], il[...] = split(inv_ref[...])

    @pl.loop(0, nc)
    def _(q):
        @pl.when(z < r)
        def _():
            share(1, q).wait_recv()
            s[q] = s[q] + dot3(lh[...], ll[...], xs[q])
            exchange(q).start()
            exchange(q).wait_recv()
            fo[q] = s[q, mine] + ex[q]

            @pl.when(z > 0)
            def _():
                chain(q, fin, f_r, partner).wait_recv()
                fo[q] = fo[q] + fin[q]

            chain(q, fin, f_r, c + 2).start()

        @pl.when(z == r)
        def _():
            exchange(q).wait_recv()
            fo[q] = s[q, mine] + ex[q]

            @pl.when(z > 0)
            def _():
                chain(q, fin, f_r, partner).wait_recv()
                fo[q] = fo[q] + fin[q]

            @pl.when(z < planes - 1)
            def _():
                chain(q, back, b_r, partner).wait_recv()
                fo[q] = fo[q] + back[q]

            xs[q] = dot3(ih[...], il[...], -fo[q])

            @pl.when(k == 0)
            def _():
                s[q, other] = s[q, other] + dot3(lh[h:], ll[h:], xs[q])
                exchange(q).start()

            @pl.loop(1, nr)
            def _(i):
                share(i, q).start()

            @pl.when(q == c)
            def _():
                xo[mine] = xs[q]

            @pl.when(q != c)
            def _():
                deliver(q, q).start()

    @pl.loop(0, nc)
    def _(q):
        exchange(q).wait_send()

        @pl.when(z > r)
        def _():
            share(1, q).wait_recv()

        @pl.when(z != r)
        def _():
            chain(q, fin, f_r, partner).wait_send()

        @pl.when(z == r)
        def _():
            @pl.loop(1, nr)
            def _(i):
                share(i, q).wait_send()

            @pl.when(q != c)
            def _():
                deliver(q, partner).wait_send()

    for half in range(2):
        @pl.when(c != 2 * r + half)
        def _():
            remote(
                xs.at[0], xo.at[pl.ds(half * h, h)], o_s.at[0], o_r.at[half], (r, partner)
            ).wait_recv()

    out_ref[...] = xo[...]
    panel_ref[...] = xs[...]


def body(l_rows, v_prev, l_tail, k_cross, k_query):
    nr, nc = lax.axis_size("row"), lax.axis_size("col")
    tr, tc = l_tail.shape
    tm = l_rows.shape[1]
    w = k_cross.shape[1]
    assert tr == 2 * tc and nc == 2 * nr
    query = w * nc
    r, c = lax.axis_index("row"), lax.axis_index("col")

    v_chunks = v_prev.reshape(tm, nc // nr, w).transpose(1, 0, 2)
    v_all = lax.all_gather(v_chunks, "row", axis=0, tiled=True)
    inverse = invert(lax.dynamic_slice_in_dim(l_tail, (c % 2) * tc, tc, 0))

    vmem = pl.BlockSpec(memory_space=pltpu.VMEM)
    own_block, panel = pl.pallas_call(
        functools.partial(solve_kernel, nr, nc),
        out_shape=(
            jax.ShapeDtypeStruct((tr, w), F32),
            jax.ShapeDtypeStruct((nc, tc, w), F32),
        ),
        in_specs=[vmem] * 5,
        out_specs=(vmem, vmem),
        scratch_shapes=[
            pltpu.VMEM((tr, tm), BF16), pltpu.VMEM((tr, tm), BF16),
            pltpu.VMEM((tr, tc), BF16), pltpu.VMEM((tr, tc), BF16),
            pltpu.VMEM((tc, tc), BF16), pltpu.VMEM((tc, tc), BF16),
            pltpu.VMEM((nc, tr, w), F32),
        ] + [pltpu.VMEM((nc, tc, w), F32)] * 5 + [
            pltpu.VMEM((tr, w), F32),
        ] + [pltpu.SemaphoreType.DMA((nc,))] * 5 + [
            pltpu.SemaphoreType.DMA((nr, nc)),
            pltpu.SemaphoreType.DMA((nc,)),
            pltpu.SemaphoreType.DMA((nc,)),
            pltpu.SemaphoreType.DMA((2,)),
        ],
        compiler_params=pltpu.CompilerParams(
            collective_id=0, has_side_effects=True, vmem_limit_bytes=48 * 2**20
        ),
        cost_estimate=pl.CostEstimate(
            flops=12 * tr * tc * query, bytes_accessed=8 * tr * query, transcendentals=0
        ),
    )(l_rows, v_all, l_tail, inverse, k_cross)

    stacked = jnp.concatenate([v_all, panel], axis=1)
    stacked = stacked.transpose(1, 0, 2).reshape(tm + tc, query)
    rows = query // nr
    left = lax.dynamic_slice_in_dim(stacked, r * rows, rows, 1)
    gram = exact_dot(left.T, stacked)
    gram = lax.psum_scatter(gram, "col", scatter_dimension=1, tiled=True)
    return (own_block, k_query - gram)


def solution(mesh):
    in_specs = (P("row", "col"), P("col", "row"), P("row", "col"), P("row", "col"), P("row", "col"))
    out_specs = (P("row", "col"), P("row", "col"))
    return jax.shard_map(body, mesh=mesh, in_specs=in_specs, out_specs=out_specs, check_vma=False)
```

time: 1130 us -> 287 us (0.25)
  waiting for transfers between devices: 904 us -> 124 us
  Pallas kernels: 0 us -> 128 us
  other arithmetic: 105 us -> 3.83 us
  matrix products: 65.8 us -> 7.19 us
  local copies, waits for them, and re-layouts: 35.8 us -> 9.69 us
    psum x4 -> x0, waiting for transfers between devices: 580 us -> none  [spread(): return lax.psum(jnp.where(mine, value, jnp.zeros_like(value)), axis)]
    all_gather x3 -> x1, waiting for transfers between devices: 240 us -> 32.9 us  [body(): v_all = lax.all_gather(v_chunks, 'row', axis=0, tiled=True)]
    pallas_call x0 -> x2, Pallas kernels: none -> 128 us  [the longest x1 123 us: body(): pl.pallas_call(functools.partial(solve_kernel, nr, nc), out_shape=(jax.Sh...]
    another operation x3 -> x0, other arithmetic: 84.8 us -> none  [solve_block(): jax.scipy.linalg.solve_triangular(diagonal_block, right_side, lower=True)]
    dot_general x7 -> x1, matrix products: 46.6 us -> 7.19 us  [exact_dot(): jnp.dot(a, b, precision=lax.Precision.HIGHEST, preferred_element_type=F32)]
    another operation x25 -> x0, local copies, waits for them, and re-layouts: 28.7 us -> none
    another operation x15 -> x0, matrix products: 19.2 us -> none  [solve_block(): jax.scipy.linalg.solve_triangular(diagonal_block, right_side, lower=True)]
    reduce_scatter x2 -> x1, waiting for transfers between devices: 82.5 us -> 91.3 us  [body(): gram = lax.psum_scatter(gram, 'col', scatter_dimension=1, tiled=True)]
  transfers between devices with their start and end apart: 9 -> 2, of which waited for: 9 -> 2; matrix products, arithmetic and copies ran while one was open for 0% -> 0% of each run, Pallas kernels for 0% -> 2%
where the time goes in v1:
time: 287 us
  Pallas kernels  128 us (45%)
  waiting for transfers between devices  124 us (43%)
  between operations  14.1 us (5%)
  local copies, waits for them, and re-layouts  9.69 us (3%)
  matrix products  7.19 us (3%)
  other arithmetic  3.83 us (1%)
    pallas_call x1, Pallas kernels, body(): pl.pallas_call(functools.partial(solve_kernel, nr, nc), out_shape=(jax.Sh...  123 us
    reduce_scatter x1, waiting for transfers between devices, body(): gram = lax.psum_scatter(gram, 'col', scatter_dimension=1, tiled=True)  91.3 us
    all_gather x1, waiting for transfers between devices, body(): v_all = lax.all_gather(v_chunks, 'row', axis=0, tiled=True)  32.9 us
    dot_general x1, matrix products, exact_dot(): jnp.dot(a, b, precision=lax.Precision.HIGHEST, preferred_element_type=F32)  7.19 us
  transfers between devices with their start and end apart: 2, of which 2 were waited for; matrix products, arithmetic and copies ran while one was open for 0% of the time, Pallas kernels for 2%

profile of v1, /device:TPU:0, one launch (start us, length us, event | category | flops | bytes accessed | tf_op | source)
XLA Modules:
  0.0 286.8 jit_solution(14389341835584669080)
XLA Ops:
  7.2 0.0 all-gather.2.cloned.1.call-start
  7.2 1.2 copy.10
  8.5 1.0 copy.11
  9.5 0.0 all-gather.2.cloned.1.call-update
  9.5 0.0 reduce-scatter.2.cloned.1.call-start
  9.5 1.3 constant_dynamic-slice_fusion.block_ref
  10.8 0.0 copy-start
  10.9 4.7 %shard_map.68.inv_ref = f32[512,512]{1,0:T(8,128)S(1)} custom-call(f32[512,512]{1,0:T(8,128)S(1)} %constant_dynamic-slice_fusion.block_ref), custom_call_target="tpu_custom_call" | custom-call | flops 2684354560 | bytes 2097152 | tf_op jit(solution)/shard_map/pallas_call | solution.py:56
  15.5 32.9 %all-gather.2.cloned.1.call-done.v_ref = f32[8,512,128]{2,1,0:T(8,128)} async-done(((f32[2,512,128]{2,1,0:T(8,128)}), f32[8,512,128]{2,1,0:T(8,128)}) %all-gather.2.cloned.1.call-update) | async-done | bytes 2097168 | tf_op jit(solution)/shard_map/all_gather | solution.py:236
  48.5 0.0 copy-done
  48.5 0.0 copy-start.1
  48.5 123.0 %shard_map.69 = (f32[1024,128]{1,0:T(8,128)S(1)}, f32[8,512,128]{2,1,0:T(8,128)S(1)}) custom-call(f32[1024,512]{1,0:T(8,128)} %lr_ref.1, f32[8,512,128]{2,1,0:T(8,128)} %all-gather.2.cloned.1.call-done.v_ref, f32[1024,512]{1,0:T(8,128)} %lt_ref.1, f32[512,512]{1,0:T(8,128)S(1)} %shard_map.68.inv_ref, f32[1024,128]{1,0:T(8,128)S(1)} %copy-done), custom_call_target="tpu_custom_call" | custom-call | flops 6442450944 | bytes 8388608 | tf_op jit(solution)/shard_map/pallas_call | solution.py:240
  171.5 0.0 copy-done.1
  171.5 2.3 maximum_bitcast_fusion
  173.7 5.4 %copy.12 = f32[1024,8,128]{0,2,1:T(8,128)} copy(f32[1024,8,128]{2,0,1:T(8,128)} %maximum_bitcast_fusion) | data formatting | bytes 8388608 | tf_op jit(solution)/shard_map/transpose | solution.py:270
  179.1 0.0 copy-start.2
  179.1 7.2 %fusion = f32[256,1024]{1,0:T(8,128)} fusion(f32[1024,1024]{0,1:T(8,128)} %bitcast.7, s32[]{:T(128)S(6)} %select_n.15), kind=kOutput, calls=%fused_computation.1 | convolution fusion | flops 3221225472 | bytes 6291460 | tf_op jit(solution)/shard_map/dot_general | solution.py:28
  186.3 0.0 reduce-scatter.2.cloned.1.call-update
  186.3 91.3 %reduce-scatter.2.cloned.1.call-done = f32[256,128]{1,0:T(8,128)} async-done(((f32[256,1024]{1,0:T(8,128)}), f32[256,128]{1,0:T(8,128)}) %reduce-scatter.2.cloned.1.call-update) | async-done | bytes 131088 | tf_op jit(solution)/shard_map/reduce_scatter | solution.py:274
  277.6 0.0 copy-done.2
  277.6 1.6 sub.3
  279.2 0.8 copy.14
Async XLA Ops:
  7.2 41.3 %all-gather.2.cloned.1.call-start = ((), (), s32[]{:S(2)}) async-start(), calls=%async_computation.1 | async-start | bytes 2621440 | tf_op jit(solution)/shard_map/all_gather | solution.py:236
  9.5 268.2 %reduce-scatter.2.cloned.1.call-start = ((), (), s32[]{:S(2)}) async-start(), calls=%async_computation.2 | async-start | bytes 1179648 | tf_op jit(solution)/shard_map/reduce_scatter | solution.py:274
  10.8 37.6 %copy-start = (f32[1024,128]{1,0:T(8,128)S(1)}, f32[1024,128]{1,0:T(8,128)}, u32[]{:S(2)}) copy-start(f32[1024,128]{1,0:T(8,128)} %kc_ref.1) | copy-start | bytes 1572868
  48.5 123.0 %copy-start.1 = (f32[8,512,128]{2,1,0:T(8,128)S(1)}, f32[8,512,128]{2,1,0:T(8,128)}, u32[]{:S(2)}) copy-start(f32[8,512,128]{2,1,0:T(8,128)} %all-gather.2.cloned.1.call-done.v_ref) | copy-start | bytes 6291460
  179.1 98.5 %copy-start.2 = (f32[256,128]{1,0:T(8,128)S(1)}, f32[256,128]{1,0:T(8,128)}, u32[]{:S(2)}) copy-start(f32[256,128]{1,0:T(8,128)} %param.9) | copy-start | bytes 393220
Sparse Core Ops, SparseCore 0:
  10.4 38.0 all-gather.1
  186.4 91.1 reduce-scatter.1

commit v2 on v1

--- a/solution.py
+++ b/solution.py
@@ -24,12 +24,25 @@
     return total + jnp.dot(low, value_high, preferred_element_type=F32)
 
 
+def start(copy):
+    copy.start()
+
+
+def wait_send(copy):
+    copy.wait_send()
+
+
+def grid_of(count):
+    side = max(i for i in range(1, count + 1) if count % i == 0 and i * i <= count)
+    return side, count // side
+
+
 def exact_dot(a, b):
     return jnp.dot(a, b, precision=lax.Precision.HIGHEST, preferred_element_type=F32)
 
 
-def invert_kernel(base, block_ref, out_ref):
-    order = block_ref.shape[0]
+def invert(base, block_ref, out_ref):
+    order = out_ref.shape[0]
     rows = lax.broadcasted_iota(jnp.int32, (base, base), 0)
     cols = lax.broadcasted_iota(jnp.int32, (base, base), 1)
     blocks = [block_ref[pl.ds(i, base), pl.ds(i, base)] for i in range(0, order, base)]
@@ -51,22 +64,10 @@
         size *= 2
 
 
-def invert(block):
-    order = block.shape[0]
-    return pl.pallas_call(
-        functools.partial(invert_kernel, min(order, 128)),
-        out_shape=jax.ShapeDtypeStruct(block.shape, F32),
-        in_specs=[pl.BlockSpec(memory_space=pltpu.VMEM)],
-        out_specs=pl.BlockSpec(memory_space=pltpu.VMEM),
-        compiler_params=pltpu.CompilerParams(vmem_limit_bytes=32 * 2**20),
-        cost_estimate=pl.CostEstimate(flops=20 * order**3, bytes_accessed=8 * order * order, transcendentals=0),
-    )(block)
-
-
 def solve_kernel(
-    nr, nc, lr_ref, v_ref, lt_ref, inv_ref, kc_ref, out_ref, panel_ref,
-    rh, rl, lh, ll, ih, il, s, ex, fin, back, xs, fo, xo,
-    ex_s, ex_r, c_s, f_r, b_r, x_s, x_r, o_s, o_r,
+    nr, nc, lr_ref, v_ref, lt_ref, kc_ref, out_ref, panel_ref, v_out_ref,
+    rh, rl, lh, ll, inv, ih, il, s, ex, fin, back, xs, fo, vs, xo,
+    ex_s, ex_r, c_s, f_r, b_r, o_s, o_r, x_s, x_r, v_s, v_r,
 ):
     r, c = lax.axis_index("row"), lax.axis_index("col")
     h = xs.shape[1]
@@ -99,37 +100,76 @@
     def chain(q, dst, recv, target):
         return remote(fo.at[q], dst.at[q], c_s.at[q], recv.at[q], (r, target))
 
-    def share(i, q):
-        return remote(xs.at[q], xs.at[q], x_s.at[i, q], x_r.at[q], ((r + i) % nr, c))
+    ga, gb = grid_of(nr)
+    a, b = r // gb, r % gb
+
+    def halves(buf, sends, recvs, q, half, along, i):
+        rows = buf.shape[1] // 2
+        part = pl.ds(half * rows, rows)
+        row, slot = (a * gb + (b + i) % gb, i - 1) if along else (((a + i) % ga) * gb + b, gb - 2 + i)
+        return remote(
+            buf.at[q, part], buf.at[q, part], sends.at[slot, half, q], recvs.at[half, q], (row, c)
+        )
+
+    def from_source(group, q, act):
+        for half in range(2):
+            for i in range(1, gb):
+                act(halves(*group, q, half, True, i))
+            for i in range(1, ga):
+                act(halves(*group, q, 1 - half, False, i))
+
+    def pass_on(group, q, half, act):
+        for i in range(1, gb if half else ga):
+            act(halves(*group, q, half, bool(half), i))
+
+    def arrived(group, q, half):
+        halves(*group, q, half, gb > 1, 1).wait_recv()
+
+    def receive(group, q, src):
+        @pl.when((a == src // gb) & (b != src % gb))
+        def _():
+            arrived(group, q, 0)
+            pass_on(group, q, 0, start)
+            arrived(group, q, 1)
+
+        @pl.when((a != src // gb) & (b == src % gb))
+        def _():
+            arrived(group, q, 1)
+            pass_on(group, q, 1, start)
+            arrived(group, q, 0)
+
+        @pl.when((a != src // gb) & (b != src % gb))
+        def _():
+            arrived(group, q, 0)
+            arrived(group, q, 1)
+
+    def sent(group, q, src):
+        @pl.when(r == src)
+        def _():
+            from_source(group, q, wait_send)
+
+        @pl.when((a == src // gb) & (b != src % gb))
+        def _():
+            pass_on(group, q, 0, wait_send)
+
+        @pl.when((a != src // gb) & (b == src % gb))
+        def _():
+            pass_on(group, q, 1, wait_send)
+
+    solved, prior = (xs, x_s, x_r), (vs, v_s, v_r)
+    per = nc // nr
+
+    def turn(t):
+        return (t % nr) * per + t // nr
 
     def deliver(q, target):
         return remote(xs.at[q], xo.at[mine], o_s.at[q], o_r.at[k], (r, target))
 
+    for i in range(per):
+        vs[r * per + i] = v_ref[i]
+        from_source(prior, r * per + i, start)
+
     rh[...], rl[...] = split(lr_ref[...])
-
-    @pl.loop(0, nc)
-    def _(q):
-        s[q] = dot3(rh[...], rl[...], v_ref[q])
-
-        @pl.when(q == c)
-        def _():
-            s[q] = s[q] - kc_ref[...]
-
-        @pl.when((z > r) | ((z == r) & (k == 1)))
-        def _():
-            exchange(q).start()
-
-        @pl.when(z > r)
-        def _():
-            exchange(q).wait_recv()
-            fo[q] = s[q, mine] + ex[q]
-
-            @pl.when(z < planes - 1)
-            def _():
-                chain(q, back, b_r, partner).wait_recv()
-                fo[q] = fo[q] + back[q]
-
-            chain(q, back, b_r, c - 2).start()
 
     @pl.when(z <= r)
     def _():
@@ -137,13 +177,46 @@
 
     @pl.when(z == r)
     def _():
-        ih[...], il[...] = split(inv_ref[...])
+        for half in range(2):
+            @pl.when(k == half)
+            def _():
+                invert(min(h, 128), lt_ref.at[pl.ds(half * h, h)], inv)
+
+        ih[...], il[...] = split(inv[...])
 
     @pl.loop(0, nc)
-    def _(q):
+    def _(t):
+        q = turn(t)
+        receive(prior, q, q // per)
+        s[q] = dot3(rh[...], rl[...], vs[q])
+
+        @pl.when(q == c)
+        def _():
+            s[q] = s[q] - kc_ref[...]
+
+        @pl.when((z > r) | ((z == r) & (k == 1)))
+        def _():
+            exchange(q).start()
+
+        @pl.when(z > r)
+        def _():
+            exchange(q).wait_recv()
+            fo[q] = s[q, mine] + ex[q]
+
+            @pl.when(z < planes - 1)
+            def _():
+                chain(q, back, b_r, partner).wait_recv()
+                fo[q] = fo[q] + back[q]
+
+            chain(q, back, b_r, c - 2).start()
+
+    @pl.loop(0, nc)
+    def _(t):
+        q = turn(t)
+        receive(solved, q, z)
+
         @pl.when(z < r)
         def _():
-            share(1, q).wait_recv()
             s[q] = s[q] + dot3(lh[...], ll[...], xs[q])
             exchange(q).start()
             exchange(q).wait_recv()
@@ -173,14 +246,12 @@
 
             xs[q] = dot3(ih[...], il[...], -fo[q])
 
+            from_source(solved, q, start)
+
             @pl.when(k == 0)
             def _():
                 s[q, other] = s[q, other] + dot3(lh[h:], ll[h:], xs[q])
                 exchange(q).start()
-
-            @pl.loop(1, nr)
-            def _(i):
-                share(i, q).start()
 
             @pl.when(q == c)
             def _():
@@ -194,9 +265,8 @@
     def _(q):
         exchange(q).wait_send()
 
-        @pl.when(z > r)
-        def _():
-            share(1, q).wait_recv()
+        sent(prior, q, q // per)
+        sent(solved, q, z)
 
         @pl.when(z != r)
         def _():
@@ -204,10 +274,6 @@
 
         @pl.when(z == r)
         def _():
-            @pl.loop(1, nr)
-            def _(i):
-                share(i, q).wait_send()
-
             @pl.when(q != c)
             def _():
                 deliver(q, partner).wait_send()
@@ -221,6 +287,7 @@
 
     out_ref[...] = xo[...]
     panel_ref[...] = xs[...]
+    v_out_ref[...] = vs[...]
 
 
 def body(l_rows, v_prev, l_tail, k_cross, k_query):
@@ -230,41 +297,42 @@
     w = k_cross.shape[1]
     assert tr == 2 * tc and nc == 2 * nr
     query = w * nc
-    r, c = lax.axis_index("row"), lax.axis_index("col")
+    r = lax.axis_index("row")
+    slots = sum(grid_of(nr)) - 2
 
     v_chunks = v_prev.reshape(tm, nc // nr, w).transpose(1, 0, 2)
-    v_all = lax.all_gather(v_chunks, "row", axis=0, tiled=True)
-    inverse = invert(lax.dynamic_slice_in_dim(l_tail, (c % 2) * tc, tc, 0))
 
     vmem = pl.BlockSpec(memory_space=pltpu.VMEM)
-    own_block, panel = pl.pallas_call(
+    own_block, panel, v_all = pl.pallas_call(
         functools.partial(solve_kernel, nr, nc),
         out_shape=(
             jax.ShapeDtypeStruct((tr, w), F32),
             jax.ShapeDtypeStruct((nc, tc, w), F32),
+            jax.ShapeDtypeStruct((nc, tm, w), F32),
         ),
-        in_specs=[vmem] * 5,
-        out_specs=(vmem, vmem),
+        in_specs=[vmem] * 4,
+        out_specs=(vmem, vmem, vmem),
         scratch_shapes=[
             pltpu.VMEM((tr, tm), BF16), pltpu.VMEM((tr, tm), BF16),
             pltpu.VMEM((tr, tc), BF16), pltpu.VMEM((tr, tc), BF16),
+            pltpu.VMEM((tc, tc), F32),
             pltpu.VMEM((tc, tc), BF16), pltpu.VMEM((tc, tc), BF16),
             pltpu.VMEM((nc, tr, w), F32),
         ] + [pltpu.VMEM((nc, tc, w), F32)] * 5 + [
+            pltpu.VMEM((nc, tm, w), F32),
             pltpu.VMEM((tr, w), F32),
-        ] + [pltpu.SemaphoreType.DMA((nc,))] * 5 + [
-            pltpu.SemaphoreType.DMA((nr, nc)),
-            pltpu.SemaphoreType.DMA((nc,)),
-            pltpu.SemaphoreType.DMA((nc,)),
+        ] + [pltpu.SemaphoreType.DMA((nc,))] * 6 + [
             pltpu.SemaphoreType.DMA((2,)),
-        ],
+        ] + [
+            pltpu.SemaphoreType.DMA((slots, 2, nc)), pltpu.SemaphoreType.DMA((2, nc)),
+        ] * 2,
         compiler_params=pltpu.CompilerParams(
             collective_id=0, has_side_effects=True, vmem_limit_bytes=48 * 2**20
         ),
         cost_estimate=pl.CostEstimate(
             flops=12 * tr * tc * query, bytes_accessed=8 * tr * query, transcendentals=0
         ),
-    )(l_rows, v_all, l_tail, inverse, k_cross)
+    )(l_rows, v_chunks, l_tail, k_cross)
 
     stacked = jnp.concatenate([v_all, panel], axis=1)
     stacked = stacked.transpose(1, 0, 2).reshape(tm + tc, query)

time: 287 us -> 227 us (0.79)
  Pallas kernels: 128 us -> 94.5 us
  waiting for transfers between devices: 124 us -> 98.9 us
    all_gather x1 -> x0, waiting for transfers between devices: 32.9 us -> none  [body(): v_all = lax.all_gather(v_chunks, 'row', axis=0, tiled=True)]
    pallas_call x1, Pallas kernels: 123 us -> 94.5 us  [body(): pl.pallas_call(functools.partial(solve_kernel, nr, nc), out_shape=(jax.Sh...]
    reduce_scatter x1, waiting for transfers between devices: 91.3 us -> 98.9 us  [body(): gram = lax.psum_scatter(gram, 'col', scatter_dimension=1, tiled=True)]
    pallas_call x1 -> x0, Pallas kernels: 4.69 us -> none  [invert(): pl.pallas_call(functools.partial(invert_kernel, min(order, 128)), out_sha...]
  transfers between devices with their start and end apart: 2 -> 1, of which waited for: 2 -> 1; matrix products, arithmetic and copies ran while one was open for 0% -> 0% of each run, Pallas kernels for 2% -> 0%
where the time goes in v2:
time: 227 us
  waiting for transfers between devices  98.9 us (44%)
  Pallas kernels  94.5 us (42%)
  between operations  14.1 us (6%)
  local copies, waits for them, and re-layouts  8.62 us (4%)
  matrix products  7.2 us (3%)
  other arithmetic  3.81 us (2%)
    reduce_scatter x1, waiting for transfers between devices, body(): gram = lax.psum_scatter(gram, 'col', scatter_dimension=1, tiled=True)  98.9 us
    pallas_call x1, Pallas kernels, body(): pl.pallas_call(functools.partial(solve_kernel, nr, nc), out_shape=(jax.Sh...  94.5 us
    dot_general x1, matrix products, exact_dot(): jnp.dot(a, b, precision=lax.Precision.HIGHEST, preferred_element_type=F32)  7.2 us
    transpose x1, local copies, waits for them, and re-layouts, body(): stacked = stacked.transpose(1, 0, 2).reshape(tm + tc, query)  5.35 us
  transfers between devices with their start and end apart: 1, of which 1 were waited for; matrix products, arithmetic and copies ran while one was open for 0% of the time, Pallas kernels for 0%

profile of v2, /device:TPU:0, one launch (start us, length us, event | category | flops | bytes accessed | tf_op | source)
XLA Modules:
  0.0 227.1 jit_solution(17666555446088947543)
XLA Ops:
  7.2 0.0 reduce-scatter.2.cloned.1.call-start
  7.2 1.2 copy.7
  8.5 0.2 copy.8
  8.7 0.0 copy-start
  8.7 1.0 copy-done
  9.7 94.5 %shard_map.68 = (f32[1024,128]{1,0:T(8,128)S(1)}, f32[8,512,128]{2,1,0:T(8,128)S(1)}, f32[8,512,128]{2,1,0:T(8,128)S(1)}) custom-call(f32[1024,512]{1,0:T(8,128)} %lr_ref.1, f32[2,512,128]{2,1,0:T(8,128)S(1)} %bitcast.6, f32[1024,512]{1,0:T(8,128)} %lt_ref.1, f32[1024,128]{1,0:T(8,128)S(1)} %copy-done), custom_call_target="tpu_custom_call" | custom-call | flops 6442450944 | bytes 8388608 | tf_op jit(solution)/shard_map/pallas_call | solution.py:306
  104.2 2.2 maximum_bitcast_fusion
  106.4 5.4 %copy.9 = f32[1024,8,128]{0,2,1:T(8,128)} copy(f32[1024,8,128]{2,0,1:T(8,128)} %maximum_bitcast_fusion) | data formatting | bytes 8388608 | tf_op jit(solution)/shard_map/transpose | solution.py:338
  111.8 0.0 copy-start.1
  111.8 7.2 %fusion = f32[256,1024]{1,0:T(8,128)} fusion(f32[1024,1024]{0,1:T(8,128)} %bitcast.7, s32[]{:T(128)S(6)} %select_n.3), kind=kOutput, calls=%fused_computation.1 | convolution fusion | flops 3221225472 | bytes 6291460 | tf_op jit(solution)/shard_map/dot_general | solution.py:41
  119.0 0.0 reduce-scatter.2.cloned.1.call-update
  119.0 98.9 %reduce-scatter.2.cloned.1.call-done = f32[256,128]{1,0:T(8,128)} async-done(((f32[256,1024]{1,0:T(8,128)}), f32[256,128]{1,0:T(8,128)}) %reduce-scatter.2.cloned.1.call-update) | async-done | bytes 131088 | tf_op jit(solution)/shard_map/reduce_scatter | solution.py:342
  217.9 0.0 copy-done.1
  217.9 1.6 sub.3
  219.4 0.8 copy.11
Async XLA Ops:
  7.2 210.7 %reduce-scatter.2.cloned.1.call-start = ((), (), s32[]{:S(2)}) async-start(), calls=%async_computation.1 | async-start | bytes 1179648 | tf_op jit(solution)/shard_map/reduce_scatter | solution.py:342
  8.7 1.0 copy-start
  111.8 106.1 %copy-start.1 = (f32[256,128]{1,0:T(8,128)S(1)}, f32[256,128]{1,0:T(8,128)}, u32[]{:S(2)}) copy-start(f32[256,128]{1,0:T(8,128)} %param.9) | copy-start | bytes 393220
Sparse Core Ops, SparseCore 0:
  119.1 98.6 reduce-scatter.1

commit v3 on v2

--- a/solution.py
+++ b/solution.py
@@ -65,9 +65,9 @@
 
 
 def solve_kernel(
-    nr, nc, lr_ref, v_ref, lt_ref, kc_ref, out_ref, panel_ref, v_out_ref,
-    rh, rl, lh, ll, inv, ih, il, s, ex, fin, back, xs, fo, vs, xo,
-    ex_s, ex_r, c_s, f_r, b_r, o_s, o_r, x_s, x_r, v_s, v_r,
+    nr, nc, lr_ref, v_ref, lt_ref, kc_ref, kq_ref, out_ref, post_ref,
+    rh, rl, lh, ll, inv, ih, il, th, tl, yh, yl, s, ex, fin, back, xs, fo, vs, xo, g, gx, gin,
+    ex_s, ex_r, c_s, f_r, b_r, o_s, o_r, x_s, x_r, v_s, v_r, gx_s, gx_r, g_s, g_r,
 ):
     r, c = lax.axis_index("row"), lax.axis_index("col")
     h = xs.shape[1]
@@ -165,8 +165,22 @@
     def deliver(q, target):
         return remote(xs.at[q], xo.at[mine], o_s.at[q], o_r.at[k], (r, target))
 
+    def pair_up(target):
+        return remote(
+            g.at[2 * target + 1 - k], gx.at[target], gx_s.at[target], gx_r.at[target], (r, partner)
+        )
+
+    def scatter(target, slot):
+        return remote(
+            g.at[2 * target + k], gin.at[slot], g_s.at[target], g_r.at[slot], (r, 2 * target + k)
+        )
+
+    def transposed(chunks):
+        return split(jnp.concatenate([chunks[r * per + i].T for i in range(per)], axis=0))
+
+    w = kc_ref.shape[1]
     for i in range(per):
-        vs[r * per + i] = v_ref[i]
+        vs[r * per + i] = v_ref[:, i * w:(i + 1) * w]
         from_source(prior, r * per + i, start)
 
     rh[...], rl[...] = split(lr_ref[...])
@@ -183,6 +197,8 @@
                 invert(min(h, 128), lt_ref.at[pl.ds(half * h, h)], inv)
 
         ih[...], il[...] = split(inv[...])
+
+    th[...], tl[...] = transposed(vs)
 
     @pl.loop(0, nc)
     def _(t):
@@ -210,6 +226,8 @@
 
             chain(q, back, b_r, c - 2).start()
 
+        g[q] = dot3(th[...], tl[...], vs[q])
+
     @pl.loop(0, nc)
     def _(t):
         q = turn(t)
@@ -261,6 +279,26 @@
             def _():
                 deliver(q, q).start()
 
+    yh[...], yl[...] = transposed(xs)
+
+    @pl.loop(0, planes)
+    def _(i):
+        target = (z + 1 + i) % planes
+        away, home = 2 * target + 1 - k, 2 * target + k
+        g[away] = g[away] + dot3(yh[...], yl[...], xs[away])
+        pair_up(target).start()
+        g[home] = g[home] + dot3(yh[...], yl[...], xs[home])
+
+    @pl.loop(0, planes)
+    def _(i):
+        target = (z + 1 + i) % planes
+        pair_up(target).wait_recv()
+        g[2 * target + k] = g[2 * target + k] + gx[target]
+
+        @pl.when(target != z)
+        def _():
+            scatter(target, z).start()
+
     @pl.loop(0, nc)
     def _(q):
         exchange(q).wait_send()
@@ -286,8 +324,17 @@
             ).wait_recv()
 
     out_ref[...] = xo[...]
-    panel_ref[...] = xs[...]
-    v_out_ref[...] = vs[...]
+    post_ref[...] = kq_ref[...] - g[c]
+
+    @pl.loop(0, planes)
+    def _(i):
+        pair_up(i).wait_send()
+
+        @pl.when(i != z)
+        def _():
+            scatter(i, z).wait_send()
+            scatter((z + 1) % planes, i).wait_recv()
+            post_ref[...] = post_ref[...] - gin[i]
 
 
 def body(l_rows, v_prev, l_tail, k_cross, k_query):
@@ -297,50 +344,44 @@
     w = k_cross.shape[1]
     assert tr == 2 * tc and nc == 2 * nr
     query = w * nc
-    r = lax.axis_index("row")
     slots = sum(grid_of(nr)) - 2
-
-    v_chunks = v_prev.reshape(tm, nc // nr, w).transpose(1, 0, 2)
+    planes, rows = nc // 2, query // nr
 
     vmem = pl.BlockSpec(memory_space=pltpu.VMEM)
-    own_block, panel, v_all = pl.pallas_call(
+    return pl.pallas_call(
         functools.partial(solve_kernel, nr, nc),
         out_shape=(
             jax.ShapeDtypeStruct((tr, w), F32),
-            jax.ShapeDtypeStruct((nc, tc, w), F32),
-            jax.ShapeDtypeStruct((nc, tm, w), F32),
+            jax.ShapeDtypeStruct(k_query.shape, F32),
         ),
-        in_specs=[vmem] * 4,
-        out_specs=(vmem, vmem, vmem),
+        in_specs=[vmem] * 5,
+        out_specs=(vmem, vmem),
         scratch_shapes=[
             pltpu.VMEM((tr, tm), BF16), pltpu.VMEM((tr, tm), BF16),
             pltpu.VMEM((tr, tc), BF16), pltpu.VMEM((tr, tc), BF16),
             pltpu.VMEM((tc, tc), F32),
             pltpu.VMEM((tc, tc), BF16), pltpu.VMEM((tc, tc), BF16),
+            pltpu.VMEM((rows, tm), BF16), pltpu.VMEM((rows, tm), BF16),
+            pltpu.VMEM((rows, tc), BF16), pltpu.VMEM((rows, tc), BF16),
             pltpu.VMEM((nc, tr, w), F32),
         ] + [pltpu.VMEM((nc, tc, w), F32)] * 5 + [
             pltpu.VMEM((nc, tm, w), F32),
             pltpu.VMEM((tr, w), F32),
+            pltpu.VMEM((nc, rows, w), F32),
+            pltpu.VMEM((planes, rows, w), F32),
+            pltpu.VMEM((planes, rows, w), F32),
         ] + [pltpu.SemaphoreType.DMA((nc,))] * 6 + [
             pltpu.SemaphoreType.DMA((2,)),
         ] + [
             pltpu.SemaphoreType.DMA((slots, 2, nc)), pltpu.SemaphoreType.DMA((2, nc)),
-        ] * 2,
+        ] * 2 + [pltpu.SemaphoreType.DMA((planes,))] * 4,
         compiler_params=pltpu.CompilerParams(
             collective_id=0, has_side_effects=True, vmem_limit_bytes=48 * 2**20
         ),
         cost_estimate=pl.CostEstimate(
             flops=12 * tr * tc * query, bytes_accessed=8 * tr * query, transcendentals=0
         ),
-    )(l_rows, v_chunks, l_tail, k_cross)
-
-    stacked = jnp.concatenate([v_all, panel], axis=1)
-    stacked = stacked.transpose(1, 0, 2).reshape(tm + tc, query)
-    rows = query // nr
-    left = lax.dynamic_slice_in_dim(stacked, r * rows, rows, 1)
-    gram = exact_dot(left.T, stacked)
-    gram = lax.psum_scatter(gram, "col", scatter_dimension=1, tiled=True)
-    return (own_block, k_query - gram)
+    )(l_rows, v_prev, l_tail, k_cross, k_query)
 
 
 def solution(mesh):

time: 227 us -> 191 us (0.84); the launches traced: 227 us -> 188 us
  waiting for transfers between devices: 98.9 us -> 0 us
  Pallas kernels: 94.5 us -> 179 us
  between operations: 14.1 us -> 0.65 us
  matrix products: 7.2 us -> 0 us
  other arithmetic: 3.81 us -> 0 us
    reduce_scatter x1 -> x0, waiting for transfers between devices: 98.9 us -> none  [body(): gram = lax.psum_scatter(gram, 'col', scatter_dimension=1, tiled=True)]
    pallas_call x1, Pallas kernels: 94.5 us -> 179 us  [body(): pl.pallas_call(functools.partial(solve_kernel, nr, nc), out_shape=(jax.Sh...]
    dot_general x1 -> x0, matrix products: 7.2 us -> none  [exact_dot(): jnp.dot(a, b, precision=lax.Precision.HIGHEST, preferred_element_type=F32)]
    transpose x1 -> x0, local copies, waits for them, and re-layouts: 5.35 us -> none  [body(): stacked = stacked.transpose(1, 0, 2).reshape(tm + tc, query)]
    unnamed x6 -> x12, local copies, waits for them, and re-layouts: 3.07 us -> 7.61 us
  transfers between devices with their start and end apart: 1 -> 0, of which waited for: 1 -> 0; matrix products, arithmetic and copies ran while one was open for 0% -> 0% of each run, Pallas kernels for 0% -> 0%
where the time goes in v3:
time: 191 us; the launch traced here: 188 us
  Pallas kernels  179 us (94%)
  local copies, waits for them, and re-layouts  7.61 us (4%)
    pallas_call x1, Pallas kernels, body(): pl.pallas_call(functools.partial(solve_kernel, nr, nc), out_shape=(jax.Sh...  179 us
    unnamed x12, local copies, waits for them, and re-layouts  7.61 us

profile of v3, /device:TPU:0, one launch (start us, length us, event | category | flops | bytes accessed | tf_op | source)
XLA Modules:
  0.0 187.6 jit_solution(17027385001550467494)
XLA Ops:
  0.6 0.0 copy-start
  0.6 1.6 copy-done
  2.2 0.0 copy-start.1
  2.2 1.6 copy-done.1
  3.8 0.0 copy-start.2
  3.8 1.0 copy-done.2
  4.9 0.0 copy-start.3
  4.9 1.0 copy-done.3
  5.9 0.0 copy-start.4
  5.9 0.9 copy-done.4
  6.8 179.4 %shard_map.68 = (f32[1024,128]{1,0:T(8,128)S(1)}, f32[256,128]{1,0:T(8,128)S(1)}) custom-call(f32[1024,512]{1,0:T(8,128)S(1)} %copy-done, f32[512,256]{1,0:T(8,128)S(1)} %copy-done.2, f32[1024,512]{1,0:T(8,128)S(1)} %copy-done.1, f32[1024,128]{1,0:T(8,128)S(1)} %copy-done.3, f32[256,128]{1,0:T(8,128)S(1)} %copy-done.4), custom_call_target="tpu_custom_call" | custom-call | flops 6442450944 | bytes 8388608 | tf_op jit(solution)/shard_map/pallas_call | solution.py:351
  186.2 0.8 copy.9
  187.0 0.7 copy.10
Async XLA Ops:
  0.6 1.6 copy-start
  2.2 1.6 copy-start.1
  3.8 1.0 copy-start.2
  4.9 1.0 copy-start.3
  5.9 0.9 copy-start.4

commit v4 on v3

--- a/solution.py
+++ b/solution.py
@@ -65,9 +65,10 @@
 
 
 def solve_kernel(
-    nr, nc, lr_ref, v_ref, lt_ref, kc_ref, kq_ref, out_ref, post_ref,
+    nr, nc, lr_hbm, v_hbm, lt_hbm, kc_hbm, kq_hbm, out_ref, post_ref,
+    lr_ref, v_ref, lt_ref, kc_ref, kq_ref,
     rh, rl, lh, ll, inv, ih, il, th, tl, yh, yl, s, ex, fin, back, xs, fo, vs, xo, g, gx, gin,
-    ex_s, ex_r, c_s, f_r, b_r, o_s, o_r, x_s, x_r, v_s, v_r, gx_s, gx_r, g_s, g_r,
+    ex_s, ex_r, c_s, f_r, b_r, o_s, o_r, x_s, x_r, v_s, v_r, gx_s, gx_r, g_s, g_r, load_s,
 ):
     r, c = lax.axis_index("row"), lax.axis_index("col")
     h = xs.shape[1]
@@ -75,7 +76,20 @@
     planes = nc // 2
     partner = c + 1 - 2 * k
     mine = pl.ds(pl.multiple_of(k * h, h), h)
-    other = pl.ds(pl.multiple_of((1 - k) * h, h), h)
+    hh = h // 2
+    pieces = [pl.ds(i * hh, hh) for i in range(2)]
+
+    def rows_of(half, p):
+        return pl.ds(pl.multiple_of(half * h + p * hh, hh), hh)
+
+    loads = [
+        pltpu.make_async_copy(src, dst, load_s.at[i])
+        for i, (src, dst) in enumerate([
+            (v_hbm, v_ref), (lr_hbm, lr_ref), (kc_hbm, kc_ref), (lt_hbm, lt_ref), (kq_hbm, kq_ref)
+        ])
+    ]
+    for load in loads:
+        load.start()
 
     barrier = pltpu.get_barrier_semaphore()
 
@@ -94,11 +108,25 @@
             src_ref=src, dst_ref=dst, send_sem=send, recv_sem=recv, device_id=device, device_id_type=MESH
         )
 
-    def exchange(q):
-        return remote(s.at[q, other], ex.at[q], ex_s.at[q], ex_r.at[q], (r, partner))
-
-    def chain(q, dst, recv, target):
-        return remote(fo.at[q], dst.at[q], c_s.at[q], recv.at[q], (r, target))
+    def exchange(q, p):
+        return remote(
+            s.at[q, rows_of(1 - k, p)], ex.at[q, pieces[p]], ex_s.at[p, q], ex_r.at[p, q], (r, partner)
+        )
+
+    def chain(q, p, dst, recv, target):
+        return remote(
+            fo.at[q, pieces[p]], dst.at[q, pieces[p]], c_s.at[p, q], recv.at[p, q], (r, target)
+        )
+
+    def gather_piece(q, p):
+        exchange(q, p).wait_recv()
+        fo[q, pieces[p]] = s[q, rows_of(k, p)] + ex[q, pieces[p]]
+
+    def add_from(q, p, dst, recv, there):
+        @pl.when(there)
+        def _():
+            chain(q, p, dst, recv, partner).wait_recv()
+            fo[q, pieces[p]] = fo[q, pieces[p]] + dst[q, pieces[p]]
 
     ga, gb = grid_of(nr)
     a, b = r // gb, r % gb
@@ -111,12 +139,12 @@
             buf.at[q, part], buf.at[q, part], sends.at[slot, half, q], recvs.at[half, q], (row, c)
         )
 
-    def from_source(group, q, act):
-        for half in range(2):
+    def from_source(group, q, act, part=(0, 1)):
+        for half in part:
             for i in range(1, gb):
                 act(halves(*group, q, half, True, i))
             for i in range(1, ga):
-                act(halves(*group, q, 1 - half, False, i))
+                act(halves(*group, q, half, False, i))
 
     def pass_on(group, q, half, act):
         for i in range(1, gb if half else ga):
@@ -179,11 +207,45 @@
         return split(jnp.concatenate([chunks[r * per + i].T for i in range(per)], axis=0))
 
     w = kc_ref.shape[1]
+    loads[0].wait()
     for i in range(per):
         vs[r * per + i] = v_ref[:, i * w:(i + 1) * w]
         from_source(prior, r * per + i, start)
 
+    loads[1].wait()
     rh[...], rl[...] = split(lr_ref[...])
+    th[...], tl[...] = transposed(vs)
+    loads[2].wait()
+
+    @pl.loop(0, nc)
+    def _(t):
+        q = turn(t)
+        receive(prior, q, q // per)
+
+        def update(half, p):
+            rows = rows_of(half, p)
+            term = dot3(rh[rows], rl[rows], vs[q])
+            s[q, rows] = term - jnp.where(q == c, kc_ref[rows], 0.0)
+
+        for p in range(2):
+            update(1 - k, p)
+
+            @pl.when((z > r) | ((z == r) & (k == 1)))
+            def _():
+                exchange(q, p).start()
+
+        for p in range(2):
+            update(k, p)
+
+            @pl.when(z > r)
+            def _():
+                gather_piece(q, p)
+                add_from(q, p, back, b_r, z < planes - 1)
+                chain(q, p, back, b_r, c - 2).start()
+
+        g[q] = dot3(th[...], tl[...], vs[q])
+
+    loads[3].wait()
 
     @pl.when(z <= r)
     def _():
@@ -198,36 +260,6 @@
 
         ih[...], il[...] = split(inv[...])
 
-    th[...], tl[...] = transposed(vs)
-
-    @pl.loop(0, nc)
-    def _(t):
-        q = turn(t)
-        receive(prior, q, q // per)
-        s[q] = dot3(rh[...], rl[...], vs[q])
-
-        @pl.when(q == c)
-        def _():
-            s[q] = s[q] - kc_ref[...]
-
-        @pl.when((z > r) | ((z == r) & (k == 1)))
-        def _():
-            exchange(q).start()
-
-        @pl.when(z > r)
-        def _():
-            exchange(q).wait_recv()
-            fo[q] = s[q, mine] + ex[q]
-
-            @pl.when(z < planes - 1)
-            def _():
-                chain(q, back, b_r, partner).wait_recv()
-                fo[q] = fo[q] + back[q]
-
-            chain(q, back, b_r, c - 2).start()
-
-        g[q] = dot3(th[...], tl[...], vs[q])
-
     @pl.loop(0, nc)
     def _(t):
         q = turn(t)
@@ -235,41 +267,36 @@
 
         @pl.when(z < r)
         def _():
-            s[q] = s[q] + dot3(lh[...], ll[...], xs[q])
-            exchange(q).start()
-            exchange(q).wait_recv()
-            fo[q] = s[q, mine] + ex[q]
-
-            @pl.when(z > 0)
-            def _():
-                chain(q, fin, f_r, partner).wait_recv()
-                fo[q] = fo[q] + fin[q]
-
-            chain(q, fin, f_r, c + 2).start()
+            def update(half, p):
+                rows = rows_of(half, p)
+                s[q, rows] = s[q, rows] + dot3(lh[rows], ll[rows], xs[q])
+
+            for p in range(2):
+                update(1 - k, p)
+                exchange(q, p).start()
+
+            for p in range(2):
+                update(k, p)
+                gather_piece(q, p)
+                add_from(q, p, fin, f_r, z > 0)
+                chain(q, p, fin, f_r, c + 2).start()
 
         @pl.when(z == r)
         def _():
-            exchange(q).wait_recv()
-            fo[q] = s[q, mine] + ex[q]
-
-            @pl.when(z > 0)
-            def _():
-                chain(q, fin, f_r, partner).wait_recv()
-                fo[q] = fo[q] + fin[q]
-
-            @pl.when(z < planes - 1)
-            def _():
-                chain(q, back, b_r, partner).wait_recv()
-                fo[q] = fo[q] + back[q]
-
-            xs[q] = dot3(ih[...], il[...], -fo[q])
-
-            from_source(solved, q, start)
+            for p in range(2):
+                gather_piece(q, p)
+                add_from(q, p, back, b_r, z < planes - 1)
+                add_from(q, p, fin, f_r, z > 0)
+                known = pl.ds(0, (p + 1) * hh)
+                xs[q, pieces[p]] = dot3(ih[pieces[p], known], il[pieces[p], known], -fo[q, known])
+                from_source(solved, q, start, (p,))
 
             @pl.when(k == 0)
             def _():
-                s[q, other] = s[q, other] + dot3(lh[h:], ll[h:], xs[q])
-                exchange(q).start()
+                for p in range(2):
+                    rows = pl.ds(h + p * hh, hh)
+                    s[q, rows] = s[q, rows] + dot3(lh[rows], ll[rows], xs[q])
+                    exchange(q, p).start()
 
             @pl.when(q == c)
             def _():
@@ -301,14 +328,16 @@
 
     @pl.loop(0, nc)
     def _(q):
-        exchange(q).wait_send()
+        for p in range(2):
+            exchange(q, p).wait_send()
 
         sent(prior, q, q // per)
         sent(solved, q, z)
 
         @pl.when(z != r)
         def _():
-            chain(q, fin, f_r, partner).wait_send()
+            for p in range(2):
+                chain(q, p, fin, f_r, partner).wait_send()
 
         @pl.when(z == r)
         def _():
@@ -324,6 +353,7 @@
             ).wait_recv()
 
     out_ref[...] = xo[...]
+    loads[4].wait()
     post_ref[...] = kq_ref[...] - g[c]
 
     @pl.loop(0, planes)
@@ -354,9 +384,11 @@
             jax.ShapeDtypeStruct((tr, w), F32),
             jax.ShapeDtypeStruct(k_query.shape, F32),
         ),
-        in_specs=[vmem] * 5,
+        in_specs=[pl.BlockSpec(memory_space=pl.ANY)] * 5,
         out_specs=(vmem, vmem),
         scratch_shapes=[
+            pltpu.VMEM(l_rows.shape, F32), pltpu.VMEM(v_prev.shape, F32), pltpu.VMEM(l_tail.shape, F32),
+            pltpu.VMEM(k_cross.shape, F32), pltpu.VMEM(k_query.shape, F32),
             pltpu.VMEM((tr, tm), BF16), pltpu.VMEM((tr, tm), BF16),
             pltpu.VMEM((tr, tc), BF16), pltpu.VMEM((tr, tc), BF16),
             pltpu.VMEM((tc, tc), F32),
@@ -370,13 +402,14 @@
             pltpu.VMEM((nc, rows, w), F32),
             pltpu.VMEM((planes, rows, w), F32),
             pltpu.VMEM((planes, rows, w), F32),
-        ] + [pltpu.SemaphoreType.DMA((nc,))] * 6 + [
+        ] + [pltpu.SemaphoreType.DMA((2, nc))] * 5 + [
+            pltpu.SemaphoreType.DMA((nc,)),
             pltpu.SemaphoreType.DMA((2,)),
         ] + [
             pltpu.SemaphoreType.DMA((slots, 2, nc)), pltpu.SemaphoreType.DMA((2, nc)),
-        ] * 2 + [pltpu.SemaphoreType.DMA((planes,))] * 4,
+        ] * 2 + [pltpu.SemaphoreType.DMA((planes,))] * 4 + [pltpu.SemaphoreType.DMA((5,))],
         compiler_params=pltpu.CompilerParams(
-            collective_id=0, has_side_effects=True, vmem_limit_bytes=48 * 2**20
+            collective_id=0, has_side_effects=True, vmem_limit_bytes=56 * 2**20
         ),
         cost_estimate=pl.CostEstimate(
             flops=12 * tr * tc * query, bytes_accessed=8 * tr * query, transcendentals=0

time: 191 us -> 193 us (1.010)
  Pallas kernels: 179 us -> 186 us
  local copies, waits for them, and re-layouts: 7.61 us -> 3.44 us
    pallas_call x1, Pallas kernels: 179 us -> 186 us  [body(): pl.pallas_call(functools.partial(solve_kernel, nr, nc), out_shape=(jax.Sh...]
    unnamed x12 -> x2, local copies, waits for them, and re-layouts: 7.61 us -> 3.44 us
where the time goes in v4:
time: 193 us; the launch traced here: 190 us
  Pallas kernels  186 us (96%)
  local copies, waits for them, and re-layouts  3.44 us (2%)
    pallas_call x1, Pallas kernels, body(): pl.pallas_call(functools.partial(solve_kernel, nr, nc), out_shape=(jax.Sh...  186 us

profile of v4, /device:TPU:0, one launch (start us, length us, event | category | flops | bytes accessed | tf_op | source)
XLA Modules:
  0.0 189.8 jit_solution(9057482673005851380)
XLA Ops:
  0.6 185.8 %shard_map.68 = (f32[1024,128]{1,0:T(8,128)}, f32[256,128]{1,0:T(8,128)}) custom-call(f32[1024,512]{1,0:T(8,128)} %lr_hbm.1, f32[512,256]{1,0:T(8,128)} %v_hbm.1, f32[1024,512]{1,0:T(8,128)} %lt_hbm.1, f32[1024,128]{1,0:T(8,128)} %kc_hbm.1, f32[256,128]{1,0:T(8,128)} %kq_hbm.1), custom_call_target="tpu_custom_call" | custom-call | flops 6442450944 | bytes 8388608 | tf_op jit(solution)/shard_map/pallas_call | solution.py:381
  186.4 1.9 copy.9
  188.3 1.6 copy.10

commit v5 on v4

--- a/solution.py
+++ b/solution.py
@@ -214,36 +214,44 @@
 
     loads[1].wait()
     rh[...], rl[...] = split(lr_ref[...])
-    th[...], tl[...] = transposed(vs)
     loads[2].wait()
 
-    @pl.loop(0, nc)
+    @pl.loop(0, nc + 1)
     def _(t):
-        q = turn(t)
-        receive(prior, q, q // per)
-
-        def update(half, p):
-            rows = rows_of(half, p)
-            term = dot3(rh[rows], rl[rows], vs[q])
-            s[q, rows] = term - jnp.where(q == c, kc_ref[rows], 0.0)
-
-        for p in range(2):
-            update(1 - k, p)
-
-            @pl.when((z > r) | ((z == r) & (k == 1)))
-            def _():
-                exchange(q, p).start()
-
-        for p in range(2):
-            update(k, p)
-
-            @pl.when(z > r)
-            def _():
+        @pl.when(t < nc)
+        def _():
+            q = turn(t)
+            receive(prior, q, q // per)
+
+            def update(half, p):
+                rows = rows_of(half, p)
+                term = dot3(rh[rows], rl[rows], vs[q])
+                s[q, rows] = term - jnp.where(q == c, kc_ref[rows], 0.0)
+
+            for p in range(2):
+                update(1 - k, p)
+
+                @pl.when((z > r) | ((z == r) & (k == 1)))
+                def _():
+                    exchange(q, p).start()
+
+            for p in range(2):
+                update(k, p)
+
+        @pl.when((z > r) & (t > 0))
+        def _():
+            q = turn(t - 1)
+            for p in range(2):
                 gather_piece(q, p)
                 add_from(q, p, back, b_r, z < planes - 1)
                 chain(q, p, back, b_r, c - 2).start()
 
-        g[q] = dot3(th[...], tl[...], vs[q])
+    def prior_gram():
+        th[...], tl[...] = transposed(vs)
+
+        @pl.loop(0, nc)
+        def _(q):
+            g[q] = dot3(th[...], tl[...], vs[q])
 
     loads[3].wait()
 
@@ -260,6 +268,8 @@
 
         ih[...], il[...] = split(inv[...])
 
+    pl.when(z > 0)(prior_gram)
+
     @pl.loop(0, nc)
     def _(t):
         q = turn(t)
@@ -306,6 +316,7 @@
             def _():
                 deliver(q, q).start()
 
+    pl.when(z == 0)(prior_gram)
     yh[...], yl[...] = transposed(xs)
 
     @pl.loop(0, planes)

time: 193 us -> 192 us (level)
  no operation moved by 1% of the time
where the time goes in v5:
time: 192 us; the launch traced here: 189 us
  Pallas kernels  185 us (96%)
  local copies, waits for them, and re-layouts  3.44 us (2%)
    pallas_call x1, Pallas kernels, body(): pl.pallas_call(functools.partial(solve_kernel, nr, nc), out_shape=(jax.Sh...  185 us

profile of v5, /device:TPU:0, one launch (start us, length us, event | category | flops | bytes accessed | tf_op | source)
XLA Modules:
  0.0 189.1 jit_solution(14837023930027422567)
XLA Ops:
  0.6 185.0 %shard_map.68 = (f32[1024,128]{1,0:T(8,128)}, f32[256,128]{1,0:T(8,128)}) custom-call(f32[1024,512]{1,0:T(8,128)} %lr_hbm.1, f32[512,256]{1,0:T(8,128)} %v_hbm.1, f32[1024,512]{1,0:T(8,128)} %lt_hbm.1, f32[1024,128]{1,0:T(8,128)} %kc_hbm.1, f32[256,128]{1,0:T(8,128)} %kq_hbm.1), custom_call_target="tpu_custom_call" | custom-call | flops 6442450944 | bytes 8388608 | tf_op jit(solution)/shard_map/pallas_call | solution.py:392
  185.7 1.9 copy.9
  187.5 1.6 copy.10

commit v6 on v5

--- a/solution.py
+++ b/solution.py
@@ -253,6 +253,29 @@
         def _(q):
             g[q] = dot3(th[...], tl[...], vs[q])
 
+    def tail_gram(first, last):
+        yh[...], yl[...] = transposed(xs)
+
+        @pl.loop(first, last)
+        def _(i):
+            target = (z + 1 + i) % planes
+            away, home = 2 * target + 1 - k, 2 * target + k
+            g[away] = g[away] + dot3(yh[...], yl[...], xs[away])
+            pair_up(target).start()
+            g[home] = g[home] + dot3(yh[...], yl[...], xs[home])
+
+        @pl.loop(first, last)
+        def _(i):
+            target = (z + 1 + i) % planes
+            pair_up(target).wait_recv()
+            g[2 * target + k] = g[2 * target + k] + gx[target]
+
+            @pl.when(target != z)
+            def _():
+                scatter(target, z).start()
+
+    early = (z == planes - 1) & (r < nr - 1)
+
     loads[3].wait()
 
     @pl.when(z <= r)
@@ -273,6 +296,11 @@
     @pl.loop(0, nc)
     def _(t):
         q = turn(t)
+
+        @pl.when(early & (t == nc - 1))
+        def _():
+            tail_gram(0, planes - 1)
+
         receive(solved, q, z)
 
         @pl.when(z < r)
@@ -317,25 +345,7 @@
                 deliver(q, q).start()
 
     pl.when(z == 0)(prior_gram)
-    yh[...], yl[...] = transposed(xs)
-
-    @pl.loop(0, planes)
-    def _(i):
-        target = (z + 1 + i) % planes
-        away, home = 2 * target + 1 - k, 2 * target + k
-        g[away] = g[away] + dot3(yh[...], yl[...], xs[away])
-        pair_up(target).start()
-        g[home] = g[home] + dot3(yh[...], yl[...], xs[home])
-
-    @pl.loop(0, planes)
-    def _(i):
-        target = (z + 1 + i) % planes
-        pair_up(target).wait_recv()
-        g[2 * target + k] = g[2 * target + k] + gx[target]
-
-        @pl.when(target != z)
-        def _():
-            scatter(target, z).start()
+    tail_gram(jnp.where(early, planes - 1, 0), planes)
 
     @pl.loop(0, nc)
     def _(q):

time: 192 us -> 188 us (0.979)
  Pallas kernels: 185 us -> 182 us
    pallas_call x1, Pallas kernels: 185 us -> 182 us  [body(): pl.pallas_call(functools.partial(solve_kernel, nr, nc), out_shape=(jax.Sh...]
where the time goes in v6:
time: 188 us; the launch traced here: 186 us
  Pallas kernels  182 us (97%)
  local copies, waits for them, and re-layouts  3.44 us (2%)
    pallas_call x1, Pallas kernels, body(): pl.pallas_call(functools.partial(solve_kernel, nr, nc), out_shape=(jax.Sh...  182 us

profile of v6, /device:TPU:0, one launch (start us, length us, event | category | flops | bytes accessed | tf_op | source)
XLA Modules:
  0.0 185.8 jit_solution(2474762214034578677)
XLA Ops:
  0.6 181.7 %shard_map.68 = (f32[1024,128]{1,0:T(8,128)}, f32[256,128]{1,0:T(8,128)}) custom-call(f32[1024,512]{1,0:T(8,128)} %lr_hbm.1, f32[512,256]{1,0:T(8,128)} %v_hbm.1, f32[1024,512]{1,0:T(8,128)} %lt_hbm.1, f32[1024,128]{1,0:T(8,128)} %kc_hbm.1, f32[256,128]{1,0:T(8,128)} %kq_hbm.1), custom_call_target="tpu_custom_call" | custom-call | flops 6442450944 | bytes 8388608 | tf_op jit(solution)/shard_map/pallas_call | solution.py:402
  182.4 1.9 %copy.9 = f32[1024,128]{1,0:T(8,128)} copy(f32[1024,128]{1,0:T(8,128)} %get-tuple-element.4) | data formatting | bytes 1048576
  184.2 1.6 copy.10
